TPU v7x, 128 devices: a whole 4x4x4 slice. The times are simulated.
128 devices in a mesh: crop: 4 (over z), scene: 32 (over x, y, core).
Axes of the slice: x: 4, y: 4, z: 4, core: 2. Of those that a mesh axis runs over, the one named last changes fastest.
Arguments:
- fine_feats: bfloat16 [4, 196608, 128], P('crop', 'scene'), may hold values from -6 to 6
- out_grad: bfloat16 [4, 196608, 128], P('crop', 'scene'), may hold values from -6 to 6
- pre_act: bfloat16 [4, 32, 32, 2, 64, 256], P('crop', 'scene'), may hold values from -6 to 6
- deep_grad: bfloat16 [4, 32, 32, 2, 64, 256], P('crop', 'scene'), may hold values from -6 to 6
- down_weight: bfloat16 [8, 128, 256], replicated, may hold values from -0.3125 to 0.3125
- up_weight: bfloat16 [8, 256, 128], replicated, may hold values from -0.375 to 0.375
- block_owner: int32 [4, 1024, 1], P('crop', 'scene'), may hold values from 0 to 31; in each aligned block of 32 rows (0 to 31, 32 to 63, ..., all dimensions but the last counted through in order) at most 2 rows name the same one
- parent_slot: int32 [4, 196608], P('crop', 'scene'), may hold values from 0 to 63, as said below
- child_offset: int32 [4, 196608], P('crop', 'scene'), may hold values from 0 to 7, as said below
Outputs:
- fine_grad: bfloat16 [4, 196608, 128], P('crop', 'scene')
- down_grad: float32 [8, 128, 256], replicated
- up_grad: float32 [8, 256, 128], replicated
- bias_grad: float32 [256], replicated
Inputs may be any that keep to these rules, and one draw needn't show every extreme that they name: `parent_slot`: within each aligned block of 192 fine sites the parent index never falls and each of the 64 parents has 1 to 8 sites. `child_offset`: offsets strictly rise within one parent. `block_owner`: among the 32 blocks of one scene index no owner is named more than 2 times, a bound that some block reaches.
All inputs are finite; a program needn't handle non-finite values.
Results may differ from a plain program's by a relative error of at most 0.005.
Values may be sent and summed in bfloat16 or wider, within the bound.
A program may use at most 128 MiB of HBM per device.

v0:
```python
import jax
import jax.numpy as jnp
from jax import lax
from jax.sharding import PartitionSpec as P


def silu_parts(pre_value):
    pre_float = pre_value.astype(jnp.float32)
    sig_value = jax.nn.sigmoid(pre_float)
    return (pre_float * sig_value, sig_value * (1.0 + pre_float * (1.0 - sig_value)))


def pick_rows(row_ids, total_rows, table):
    selector = (row_ids[:, None] == jnp.arange(total_rows, dtype=jnp.int32)[None, :]).astype(
        table.dtype
    )
    picked = jnp.dot(selector, table.reshape(total_rows, -1), preferred_element_type=jnp.float32)
    return picked.astype(table.dtype).reshape((row_ids.shape[0],) + table.shape[1:])


def local_grads(feats, cotan, places, parent_pre, parent_deep, live_rows, wu_mat, wd_mat):
    block_total, rows_block, width = feats.shape
    parents_block = parent_pre.shape[1]
    out_width = parent_pre.shape[2]
    slot_ids = jnp.arange(parents_block * 8, dtype=jnp.int32)
    chooser = (places[:, :, None] == slot_ids[None, None, :]).astype(jnp.bfloat16)
    feat_slots = (
        jnp.einsum("brs,brc->bsc", chooser, feats, preferred_element_type=jnp.float32)
        .astype(feats.dtype)
        .reshape(-1, 8 * width)
    )
    cot_slots = (
        jnp.einsum("brs,brc->bsc", chooser, cotan, preferred_element_type=jnp.float32)
        .astype(cotan.dtype)
        .reshape(-1, 8 * width)
    )
    act_value, slope_value = silu_parts(parent_pre.reshape(-1, out_width))
    act_grad = parent_deep.reshape(-1, out_width).astype(jnp.float32) + jnp.dot(
        cot_slots, wu_mat, preferred_element_type=jnp.float32
    )
    pre_grad = act_grad * slope_value
    pre_grad = jnp.where(live_rows, pre_grad, 0.0)
    pre_grad = pre_grad.astype(jnp.bfloat16)
    slot_grads = jnp.dot(pre_grad, wd_mat, preferred_element_type=jnp.float32).astype(jnp.bfloat16)
    slot_grads = slot_grads.reshape(block_total, parents_block * 8, width)
    fine_part = jnp.einsum(
        "brs,bsc->brc", chooser, slot_grads, preferred_element_type=jnp.float32
    ).astype(jnp.bfloat16)
    contract = (((0,), (0,)), ((), ()))
    up_term = lax.dot_general(
        act_value.astype(jnp.bfloat16), cot_slots, contract, preferred_element_type=jnp.float32
    )
    down_term = lax.dot_general(feat_slots, pre_grad, contract, preferred_element_type=jnp.float32)
    bias_term = jnp.sum(pre_grad.astype(jnp.float32), axis=0)
    return (fine_part, up_term, down_term, bias_term)


def on_device(
    fine_feats,
    out_grad,
    pre_act,
    deep_grad,
    down_weight,
    up_weight,
    block_owner,
    parent_slot,
    child_offset,
):
    scene_count = lax.axis_size("scene")
    crop_count = lax.axis_size("crop")
    width = fine_feats.shape[2]
    out_width = pre_act.shape[5]
    capacity = pre_act.shape[3]
    parents_block = pre_act.shape[4]
    owners = block_owner[0, :, 0]
    block_count = owners.shape[0]
    rows_block = fine_feats.shape[1] // block_count
    wu_mat = jnp.transpose(up_weight, (0, 2, 1)).reshape(8 * width, out_width)
    wd_mat = jnp.transpose(down_weight, (2, 0, 1)).reshape(out_width, 8 * width)
    earlier = jnp.arange(block_count)[None, :] < jnp.arange(block_count)[:, None]
    same_owner = owners[:, None] == owners[None, :]
    slot_rank = jnp.sum(same_owner & earlier, axis=1)
    target = owners * capacity + slot_rank
    places = (parent_slot[0] * 8 + child_offset[0]).reshape(block_count, rows_block)
    feats = fine_feats[0].reshape(block_count, rows_block, width)
    cotan = out_grad[0].reshape(block_count, rows_block, width)
    slot_total = scene_count * capacity
    holder = (
        jnp.full((slot_total,), block_count, jnp.int32)
        .at[target]
        .set(jnp.arange(block_count, dtype=jnp.int32))
    )
    feat_send = pick_rows(holder, block_count, feats).reshape(
        scene_count, capacity, rows_block, width
    )
    cot_send = pick_rows(holder, block_count, cotan).reshape(
        scene_count, capacity, rows_block, width
    )
    place_send = jnp.concatenate([places, jnp.full((1, rows_block), -1, jnp.int32)])[
        holder
    ].reshape(scene_count, capacity, rows_block)
    feat_in, cot_in = (
        lax.all_to_all(feat_send, "scene", split_axis=0, concat_axis=0, tiled=True),
        lax.all_to_all(cot_send, "scene", split_axis=0, concat_axis=0, tiled=True),
    )
    place_in = lax.all_to_all(place_send, "scene", split_axis=0, concat_axis=0, tiled=True)
    place_flat = place_in.reshape(slot_total, rows_block)
    live_rows = jnp.repeat(place_flat[:, 0] >= 0, parents_block)[:, None]
    fine_back, up_term, down_term, bias_term = local_grads(
        feat_in.reshape(slot_total, rows_block, width),
        cot_in.reshape(slot_total, rows_block, width),
        place_flat,
        pre_act[0, 0].reshape(slot_total, parents_block, out_width),
        deep_grad[0, 0].reshape(slot_total, parents_block, out_width),
        live_rows,
        wu_mat,
        wd_mat,
    )
    returned = lax.all_to_all(
        fine_back.reshape(scene_count, capacity, rows_block, width),
        "scene",
        split_axis=0,
        concat_axis=0,
        tiled=True,
    )
    fine_part = pick_rows(target, slot_total, returned.reshape(slot_total, rows_block, width))
    up_total, down_total, bias_total = lax.psum((up_term, down_term, bias_term), ("crop", "scene"))
    grad_scale = float(crop_count * scene_count * fine_feats.shape[1]) ** (-0.5)
    up_grad = jnp.transpose((up_total * grad_scale).reshape(out_width, 8, width), (1, 0, 2))
    down_grad = (down_total * grad_scale).reshape(8, width, out_width)
    return (fine_part.reshape(1, -1, width), down_grad, up_grad, bias_total * grad_scale)


def solution(mesh):
    return jax.shard_map(
        on_device,
        mesh=mesh,
        in_specs=(
            P("crop", "scene", None),
            P("crop", "scene", None),
            P("crop", "scene", None, None, None, None),
            P("crop", "scene", None, None, None, None),
            P(),
            P(),
            P("crop", "scene", None),
            P("crop", "scene"),
            P("crop", "scene"),
        ),
        out_specs=(P("crop", "scene", None), P(), P(), P()),
        check_vma=False,
    )
```

profile of v0, /device:TPU:1, one launch (start us, length us, event | category | flops | bytes accessed | tf_op | source)
XLA Modules:
  0.0 377.6 jit_solution(12867720810844927266)
XLA Ops:
  7.2 0.0 copy-start
  7.2 0.9 convert_reduce_fusion.1
  8.1 0.7 fusion.30
  8.8 0.7 scatter_custom_fusion
  9.5 0.8 add_reduce_fusion
  10.3 0.1 add.63
  10.4 0.7 gather_fusion
  11.0 0.7 reshape.93
  11.7 8.6 %all-to-all-start = ((s32[32,2,192]{2,1,0:T(2,128)}), s32[32,2,192]{2,1,0:T(2,128)S(1)}, u32[]{:S(2)}, u32[]{:S(2)}) async-start(s32[32,2,192]{2,1,0:T(2,128)} %reshape.93), calls=%async_computation | async-start | bytes 131072 | tf_op jit(solution)/shard_map/all_to_all | solution.py:106
  20.3 1.8 reshape_reshape_squeeze.8
  22.1 1.0 fusion.23
  23.2 2.5 copy.23
  25.7 2.0 all-to-all-done
  27.7 5.4 %all-to-all-start.1 = ((bf16[32,2,192,128]{3,2,1,0:T(8,128)(2,1)}), bf16[32,2,192,128]{3,2,1,0:T(8,128)(2,1)}, u32[]{:S(2)}, u32[]{:S(2)}) async-start(bf16[32,2,192,128]{3,2,1,0:T(8,128)(2,1)} %bitcast.75), calls=%async_computation.1 | async-start | bytes 6291456 | tf_op jit(solution)/shard_map/all_to_all | solution.py:104
  33.1 1.8 reshape_reshape_squeeze.9
  35.0 1.0 fusion.24
  36.0 2.5 copy.25
  38.5 34.4 %all-to-all-done.1 = bf16[32,2,192,128]{3,2,1,0:T(8,128)(2,1)} async-done(((bf16[32,2,192,128]{3,2,1,0:T(8,128)(2,1)}), bf16[32,2,192,128]{3,2,1,0:T(8,128)(2,1)}, u32[]{:S(2)}, u32[]{:S(2)}) %all-to-all-start.1) | async-done | bytes 3145760 | tf_op jit(solution)/shard_map/all_to_all | solution.py:104
  72.9 5.0 %all-to-all-start.3 = ((bf16[32,2,192,128]{3,2,1,0:T(8,128)(2,1)}), bf16[32,2,192,128]{3,2,1,0:T(8,128)(2,1)}, u32[]{:S(2)}, u32[]{:S(2)}) async-start(bf16[32,2,192,128]{3,2,1,0:T(8,128)(2,1)} %bitcast.74), calls=%async_computation.3 | async-start | bytes 6291456 | tf_op jit(solution)/shard_map/all_to_all | solution.py:103
  78.0 0.2 copy.20
  78.2 0.0 copy-start.3
  78.2 3.0 fusion.14
  81.3 3.4 fusion.19
  84.7 0.1 fusion.25
  84.8 0.1 broadcast_in_dim.36
  84.8 0.1 broadcast_in_dim.37
  84.9 13.8 %fusion.6 = bf16[64,512,128]{2,1,0:T(8,128)(2,1)} fusion(bf16[64,192,128]{2,1,0:T(8,128)(2,1)} %bitcast.5, s32[64,192]{1,0:T(8,128)S(1)} %eq.32), kind=kOutput, calls=%fused_computation.13 | convolution fusion | flops 1621098496 | bytes 11583488 | tf_op jit(solution)/shard_map/brs,brc->bsc/dot_general | solution.py:33
  98.7 13.3 %reshape.95 = bf16[4096,1024]{1,0:T(8,128)(2,1)} reshape(bf16[64,512,128]{2,1,0:T(8,128)(2,1)} %fusion.6) | data formatting | bytes 16777216 | tf_op jit(solution)/shard_map/reshape | solution.py:35
  112.0 5.8 %all-to-all-done.3 = bf16[32,2,192,128]{3,2,1,0:T(8,128)(2,1)} async-done(((bf16[32,2,192,128]{3,2,1,0:T(8,128)(2,1)}), bf16[32,2,192,128]{3,2,1,0:T(8,128)(2,1)}, u32[]{:S(2)}, u32[]{:S(2)}) %all-to-all-start.3) | async-done | bytes 3145760 | tf_op jit(solution)/shard_map/all_to_all | solution.py:103
  117.8 13.8 %fusion.7 = bf16[64,512,128]{2,1,0:T(8,128)(2,1)} fusion(bf16[64,192,128]{2,1,0:T(8,128)(2,1)} %bitcast.12, s32[64,192]{1,0:T(8,128)S(1)} %eq.32), kind=kOutput, calls=%fused_computation.14 | convolution fusion | flops 1621098496 | bytes 11583488 | tf_op jit(solution)/shard_map/brs,brc->bsc/dot_general | solution.py:28
  131.6 13.3 %reshape.101 = bf16[4096,1024]{1,0:T(8,128)(2,1)} reshape(bf16[64,512,128]{2,1,0:T(8,128)(2,1)} %fusion.7) | data formatting | bytes 16777216 | tf_op jit(solution)/shard_map/reshape | solution.py:30
  144.9 6.8 %convert_reduce_fusion = (f32[256]{0:T(256)S(1)}, bf16[4096,256]{1,0:T(8,128)(2,1)S(1)}) fusion(f32[4096,256]{1,0:T(8,128)} %fusion.19, bf16[4096,1024]{1,0:T(8,128)(2,1)} %reshape.95, bf16[1024,256]{1,0:T(8,128)(2,1)S(1)} %bitcast.78, bf16[4096,256]{1,0:T(8,128)(2,1)} %bitcast.79, pred[4096]{0:T(1024)(128)(4,1)S(1)} %broadcast_in_dim.37), kind=kOutput, calls=%fused_computation.32 | convolution fusion | flops 2154823424 | bytes 17306624 | tf_op jit(solution)/shard_map/dot_general | solution.py:38
  151.7 1.3 copy-done.1
  153.0 5.6 %convolution_convert_fusion.3 = bf16[4096,1024]{1,0:T(8,128)(2,1)} fusion(bf16[4096,256]{1,0:T(8,128)(2,1)S(1)} %get-tuple-element.7, bf16[256,1024]{0,1:T(8,128)(2,1)S(1)} %bitcast.72), kind=kOutput, calls=%fused_computation.12 | convolution fusion | flops 2151677952 | bytes 11010048 | tf_op jit(solution)/shard_map/dot_general | solution.py:44
  158.6 13.3 %reshape.98 = bf16[64,512,128]{2,1,0:T(8,128)(2,1)} reshape(bf16[4096,1024]{1,0:T(8,128)(2,1)} %convolution_convert_fusion.3) | data formatting | bytes 16777216 | tf_op jit(solution)/shard_map/reshape | solution.py:45
  171.9 8.1 %fusion.22 = bf16[64,192,128]{2,1,0:T(8,128)(2,1)} fusion(bf16[64,512,128]{2,1,0:T(8,128)(2,1)} %reshape.98, s32[64,192]{1,0:T(8,128)S(1)} %eq.32), kind=kOutput, calls=%fused_computation.35 | convolution fusion | flops 1618477056 | bytes 11583488 | tf_op jit(solution)/shard_map/brs,bsc->brc/dot_general | solution.py:46
  180.0 5.0 %all-to-all-start.2 = ((bf16[32,2,192,128]{3,2,1,0:T(8,128)(2,1)}), bf16[32,2,192,128]{3,2,1,0:T(8,128)(2,1)}, u32[]{:S(2)}, u32[]{:S(2)}) async-start(bf16[32,2,192,128]{3,2,1,0:T(8,128)(2,1)} %bitcast.76), calls=%async_computation.2 | async-start | bytes 6291456 | tf_op jit(solution)/shard_map/all_to_all | solution.py:119
  185.1 0.0 all-reduce.4.cloned.1.call-start
  185.1 6.9 %fusion.34 = f32[256,1024]{1,0:T(8,128)} fusion(bf16[4096,256]{1,0:T(8,128)(2,1)S(1)} %bitcast.73, bf16[4096,1024]{1,0:T(8,128)(2,1)} %reshape.95), kind=kOutput, calls=%fused_computation.62 | convolution fusion | flops 2147483648 | bytes 11534336 | tf_op jit(solution)/shard_map/dot_general | solution.py:50
  192.0 6.7 %fusion.33 = f32[1024,256]{1,0:T(8,128)} fusion(bf16[4096,1024]{1,0:T(8,128)(2,1)} %reshape.101, bf16[4096,256]{1,0:T(8,128)(2,1)S(1)} %copy-done.2), kind=kOutput, calls=%fused_computation.61 | convolution fusion | flops 2147483648 | bytes 11534336 | tf_op jit(solution)/shard_map/dot_general | solution.py:53
  198.7 0.0 all-reduce.4.cloned.1.call-update
  198.8 83.9 %psum.23 = f32[256]{0:T(256)S(1)} all-reduce(f32[256]{0:T(256)S(1)} %get-tuple-element.6), channel_id=1, replica_groups=mesh['crop'=4,'scene'=32] {'crop','scene'}, use_global_device_ids=true, to_apply=%region_5.6 | all-reduce | flops 256 | bytes 2048 | tf_op jit(solution)/shard_map/psum | solution.py:127
  282.7 0.6 broadcast_multiply_fusion.1
  283.2 77.2 %all-reduce.4.cloned.1.call-done = (f32[1024,256]{1,0:T(8,128)}, f32[256,1024]{1,0:T(8,128)}) async-done(((f32[1024,256]{1,0:T(8,128)}, f32[256,1024]{1,0:T(8,128)}), (f32[1024,256]{1,0:T(8,128)}, f32[256,1024]{1,0:T(8,128)})) %all-reduce.4.cloned.1.call-update) | async-done | bytes 2097168 | tf_op jit(solution)/shard_map/psum | solution.py:127
  360.4 2.3 broadcast_multiply_fusion
  362.7 2.3 bitcast_bitcast_fusion
  365.0 4.1 %convolution_convert_fusion.2 = bf16[32,24576]{1,0:T(8,128)(2,1)S(1)} fusion(bf16[8,8,192,128]{3,2,1,0:T(8,128)(2,1)} %bitcast.25, s32[32]{0:T(128)S(1)} %multiply_add_fusion), kind=kOutput, calls=%fused_computation.4 | convolution fusion | flops 101451776 | bytes 4718720 | tf_op jit(solution)/shard_map/dot_general | solution.py:17
  369.1 1.6 reshape_reshape.14
  (16 shorter events, 0.1 us)
Async XLA Ops:
  7.2 144.5 %copy-start = (bf16[8,128,256]{2,1,0:T(8,128)(2,1)S(1)}, bf16[8,128,256]{2,1,0:T(8,128)(2,1)}, u32[]{:S(2)}) copy-start(bf16[8,128,256]{2,1,0:T(8,128)(2,1)} %param.13) | copy-start | bytes 1572868
  11.7 16.0 %all-to-all-start = ((s32[32,2,192]{2,1,0:T(2,128)}), s32[32,2,192]{2,1,0:T(2,128)S(1)}, u32[]{:S(2)}, u32[]{:S(2)}) async-start(s32[32,2,192]{2,1,0:T(2,128)} %reshape.93), calls=%async_computation | async-start | bytes 131072 | tf_op jit(solution)/shard_map/all_to_all | solution.py:106
  27.7 45.3 %all-to-all-start.1 = ((bf16[32,2,192,128]{3,2,1,0:T(8,128)(2,1)}), bf16[32,2,192,128]{3,2,1,0:T(8,128)(2,1)}, u32[]{:S(2)}, u32[]{:S(2)}) async-start(bf16[32,2,192,128]{3,2,1,0:T(8,128)(2,1)} %bitcast.75), calls=%async_computation.1 | async-start | bytes 6291456 | tf_op jit(solution)/shard_map/all_to_all | solution.py:104
  38.5 39.5 %copy-start.4 = (bf16[8,256,128]{2,1,0:T(8,128)(2,1)S(1)}, bf16[8,256,128]{2,1,0:T(8,128)(2,1)}, u32[]{:S(2)}) copy-start(bf16[8,256,128]{2,1,0:T(8,128)(2,1)} %param.14) | copy-start | bytes 1572868
  72.9 44.9 %all-to-all-start.3 = ((bf16[32,2,192,128]{3,2,1,0:T(8,128)(2,1)}), bf16[32,2,192,128]{3,2,1,0:T(8,128)(2,1)}, u32[]{:S(2)}, u32[]{:S(2)}) async-start(bf16[32,2,192,128]{3,2,1,0:T(8,128)(2,1)} %bitcast.74), calls=%async_computation.3 | async-start | bytes 6291456 | tf_op jit(solution)/shard_map/all_to_all | solution.py:103
  78.2 3.0 copy-start.3
  151.7 1.3 copy-start.1
  180.0 185.0 %all-to-all-start.2 = ((bf16[32,2,192,128]{3,2,1,0:T(8,128)(2,1)}), bf16[32,2,192,128]{3,2,1,0:T(8,128)(2,1)}, u32[]{:S(2)}, u32[]{:S(2)}) async-start(bf16[32,2,192,128]{3,2,1,0:T(8,128)(2,1)} %bitcast.76), calls=%async_computation.2 | async-start | bytes 6291456 | tf_op jit(solution)/shard_map/all_to_all | solution.py:119
  185.1 175.4 %all-reduce.4.cloned.1.call-start = ((), (), s32[]{:S(2)}) async-start(), calls=%async_computation.4 | async-start | bytes 4194304 | tf_op jit(solution)/shard_map/psum | solution.py:127
  185.1 6.9 %copy-start.2 = (bf16[4096,256]{1,0:T(8,128)(2,1)S(1)}, bf16[4096,256]{1,0:T(8,128)(2,1)}, u32[]{:S(2)}) copy-start(bf16[4096,256]{1,0:T(8,128)(2,1)} %copy-done.1) | copy-start | bytes 6291460
  192.0 6.8 %copy-start.5 = (s32[1,32,1]{1,2,0:T(1,128)S(1)}, s32[1,32,1]{1,2,0:T(1,128)}, u32[]{:S(2)}) copy-start(s32[1,32,1]{1,2,0:T(1,128)} %param.15) | copy-start | bytes 388
Sparse Core Ops, SparseCore 0:
  198.9 161.4 all-reduce.3
where the time goes:
time: 379 us; the launch traced here: 378 us
  waiting for transfers between devices  119 us (31%)
  blocking collectives  83.9 us (22%)
  matrix products  67.7 us (18%)
  local copies, waits for them, and re-layouts  54.1 us (14%)
  starting transfers between devices  24.2 us (6%)
  between operations  14.2 us (4%)
  other arithmetic  14 us (4%)
    psum x1, blocking collectives, on_device(): lax.psum((up_term, down_term, bias_term), ('crop', 'scene'))  83.9 us
    psum x1, waiting for transfers between devices, on_device(): lax.psum((up_term, down_term, bias_term), ('crop', 'scene'))  77.2 us
    all_to_all x1, waiting for transfers between devices, on_device(): lax.all_to_all(cot_send, 'scene', split_axis=0, concat_axis=0, tiled=True)  34.4 us
    dot_general x1, matrix products, local_grads(): jnp.einsum('brs,brc->bsc', chooser, cotan, preferred_element_type=jnp.flo...  13.8 us
    dot_general x1, matrix products, local_grads(): jnp.einsum('brs,brc->bsc', chooser, feats, preferred_element_type=jnp.flo...  13.8 us
    reshape x1, local copies, waits for them, and re-layouts, local_grads(): slot_grads = slot_grads.reshape(block_total, parents_block * 8, width)  13.3 us
    reshape x1, local copies, waits for them, and re-layouts, local_grads(): cot_slots = jnp.einsum('brs,brc->bsc', chooser, cotan, preferred_element_...  13.3 us
    reshape x1, local copies, waits for them, and re-layouts, local_grads(): feat_slots = jnp.einsum('brs,brc->bsc', chooser, feats, preferred_element...  13.3 us
  transfers between devices with their start and end apart: 5, of which 4 were waited for; matrix products, arithmetic and copies ran while one was open for 17% of the time, Pallas kernels for 0%

commit v1 on v0

v1 whole, which is shorter than its diff:
```python
import functools

import jax
import jax.numpy as jnp
from jax import lax
from jax.experimental import pallas as pl
from jax.experimental.pallas import tpu as pltpu
from jax.sharding import PartitionSpec as P

MESH = pl.DeviceIdType.MESH
BF16 = jnp.bfloat16
F32 = jnp.float32
NT = (((1,), (0,)), ((), ()))
TN = (((0,), (0,)), ((), ()))

CHIP_ORDER = (
    (2, 1), (1, 2), (2, 3), (3, 2), (2, 2), (2, 0), (0, 2),
    (1, 3), (3, 1), (1, 1), (3, 3), (1, 0), (0, 1), (3, 0), (0, 3),
)
UPFRONT = 2


def level_kernel(
    scale,
    owner_ref, pslot_ref, coff_ref, feats_hbm, cotan_hbm, pre_hbm, deep_hbm, wd_ref, wu_ref,
    fine_out, down_out, up_out, bias_out,
    tgt, feats, cotan, recv0, recv1, recv2, recv3, chosen, cot_s, feat_t, x_s, slope_s, act_t, pg_s, wu_s, wd_s, fine_s,
    quarter, rec_a, msg_b, rec_b, part, load_sem, own_sem, x_send, x_recv,
    a_send, a_recv, b_send, b_recv, c_send, c_recv, d_send, d_recv, store_sem,
):
    recv = (recv0, recv1, recv2, recv3)
    z = lax.axis_index("crop")
    me = lax.axis_index("scene")
    chip, core = me // 2, me % 2
    cx, cy = chip // 4, chip % 4
    m = z * 2 + core

    def plane_peer(dx, dy, dc):
        return (((cx + dx) % 4) * 4 + (cy + dy) % 4) * 2 + (core + dc) % 2

    def group_peer(d):
        other = (m + d) % 8
        return other, (other // 2, chip * 2 + other % 2)

    def chip_peer(d):
        other = (chip + d) % 16
        return other, (z, other * 2 + core)

    barrier = pltpu.get_barrier_semaphore()

    def greet_plane(d, carry):
        pl.semaphore_signal(barrier, inc=1, device_id=(z, (me + d) % 32), device_id_type=MESH)
        return carry

    def greet_crops(d, carry):
        for c in range(2):
            pl.semaphore_signal(
                barrier, inc=1, device_id=((z + d) % 4, chip * 2 + c), device_id_type=MESH
            )
        return carry

    lax.fori_loop(1, 32, greet_plane, 0)
    lax.fori_loop(1, 4, greet_crops, 0)
    pl.semaphore_wait(barrier, 37)

    def source(q):
        return (pre_hbm if q < 2 else deep_hbm), pl.ds((q % 2) * 128, 128)

    def send_to(q, peer):
        ref, lanes = source(q)
        pltpu.make_async_remote_copy(
            src_ref=ref.at[pl.ds(2 * peer, 2), :, lanes],
            dst_ref=recv[q].at[pl.ds(2 * me, 2)],
            send_sem=x_send.at[q],
            recv_sem=x_recv.at[q],
            device_id=(z, peer),
            device_id_type=MESH,
        ).start()

    def own_copy(q):
        ref, lanes = source(q)
        return pltpu.make_async_copy(
            ref.at[pl.ds(2 * me, 2), :, lanes], recv[q].at[pl.ds(2 * me, 2)], own_sem.at[q]
        )

    def start_round(q):
        def half(dc, carry):
            for dx, dy in CHIP_ORDER:
                send_to(q, plane_peer(dx, dy, dc))
            return carry

        lax.fori_loop(0, 2, half, 0)
        send_to(q, plane_peer(0, 0, 1))
        own_copy(q).start()

    def bytes_of_round(q, sem):
        half = recv[q].at[pl.ds(0, 62)]
        return pltpu.make_async_copy(half, half, sem.at[q])

    def wait_round(q):
        own_copy(q).wait()
        bytes_of_round(q, x_recv).wait()

    for q in range(UPFRONT):
        start_round(q)

    loads = [
        pltpu.make_async_copy(cotan_hbm, cotan, load_sem.at[0]),
        pltpu.make_async_copy(feats_hbm, feats, load_sem.at[1]),
    ]
    for load in loads:
        load.start()

    def rank_block(b, carry):
        owner = owner_ref[b]
        count = jnp.int32(0)
        for other in range(32):
            count += jnp.where((owner_ref[other] == owner) & (other < b), 1, 0)
        tgt[b] = jnp.minimum(owner * 2 + count, 63)
        return carry

    lax.fori_loop(0, 32, rank_block, 0)

    for k in range(8):
        wu_s[pl.ds(k * 128, 128), :] = wu_ref[k].astype(F32).T.astype(BF16)
        wd_s[:, pl.ds(k * 128, 128)] = wd_ref[k].astype(F32).T.astype(BF16)
    for load in loads:
        load.wait()

    def place_pair(i, carry):
        rows, cols = [], []
        lane = lax.broadcasted_iota(jnp.int32, (1, 128), 1)
        for g in range(3):
            row = pl.ds(i * 3 + g, 1)
            place = coff_ref[row, :] * 128 + pslot_ref[row, :]
            if g == 1:
                place = place + jnp.where(lane >= 64, 64, 0)
            elif g == 2:
                place = place + 64
            sub = lax.broadcasted_iota(jnp.int32, (1024, 128), 0)
            rows.append(jnp.where(sub == place, 1.0, 0.0).astype(BF16))
            column = jnp.broadcast_to(place.astype(F32), (128, 128)).T
            lanes = lax.broadcasted_iota(jnp.int32, (128, 128), 1).astype(F32)
            for k in range(8):
                chosen[pl.ds(i * 384 + g * 128, 128), pl.ds(k * 128, 128)] = jnp.where(
                    column == lanes + float(k * 128), 1.0, 0.0
                ).astype(BF16)
        sites = pl.ds(i * 384, 384)
        parents = pl.ds(i * 128, 128)
        chooser = jnp.concatenate(rows, axis=1)
        placed = jnp.dot(chooser, cotan[sites, :], preferred_element_type=F32).astype(BF16)
        for k in range(8):
            cot_s[parents, pl.ds(k * 128, 128)] = placed[k * 128 : (k + 1) * 128, :]
        turned = lax.dot_general(
            feats[sites, :], chosen[sites, :], TN, preferred_element_type=F32
        ).astype(BF16)
        for k in range(8):
            feat_t[pl.ds(k * 128, 128), parents] = turned[:, k * 128 : (k + 1) * 128]
        return carry

    lax.fori_loop(0, 16, place_pair, 0)

    def up_tile(i, carry):
        rows = pl.ds(i * 512, 512)
        x_s[rows, :] = jnp.dot(cot_s[rows, :], wu_s[...], preferred_element_type=F32)
        return carry

    lax.fori_loop(0, 4, up_tile, 0)

    def start_a(q):
        def step(d, carry):
            other, device = group_peer(d)
            pltpu.make_async_remote_copy(
                src_ref=quarter.at[q, other], dst_ref=rec_a.at[q, m],
                send_sem=a_send.at[q], recv_sem=a_recv.at[q],
                device_id=device, device_id_type=MESH,
            ).start()
            return carry

        lax.fori_loop(1, 8, step, 0)
        rec_a[q, m] = quarter[q, m]

    def bytes_of(ref, sem):
        return pltpu.make_async_copy(ref, ref, sem)

    def next_b(q):
        bytes_of(rec_a.at[q, pl.ds(0, 7)], a_recv.at[q]).wait()
        total = rec_a[q, 0]
        for other in range(1, 8):
            total += rec_a[q, other]
        for n in range(16):
            msg_b[q, n, 0:8] = total[n * 8 : (n + 1) * 8]
            msg_b[q, n, 8:16] = total[128:136]

        def step(d, carry):
            other, device = chip_peer(d)
            pltpu.make_async_remote_copy(
                src_ref=msg_b.at[q, other], dst_ref=rec_b.at[q, chip],
                send_sem=b_send.at[q], recv_sem=b_recv.at[q],
                device_id=device, device_id_type=MESH,
            ).start()
            return carry

        lax.fori_loop(1, 16, step, 0)
        rec_b[q, chip] = msg_b[q, chip]

    def next_c(q):
        bytes_of(rec_b.at[q, pl.ds(0, 15)], b_recv.at[q]).wait()
        total = rec_b[q, 0]
        for other in range(1, 16):
            total += rec_b[q, other]
        total = total * scale
        mine = pl.ds(pl.multiple_of(chip * 8, 8), 8)
        part[q, mine] = total[0:8]
        if q >= 2:
            bias_out[:, pl.ds((q % 2) * 128, 128)] = jnp.sum(total[8:16], axis=0, keepdims=True)

        def step(d, carry):
            _, device = chip_peer(d)
            pltpu.make_async_remote_copy(
                src_ref=part.at[q, mine], dst_ref=part.at[q, mine],
                send_sem=c_send.at[q], recv_sem=c_recv.at[q],
                device_id=device, device_id_type=MESH,
            ).start()
            return carry

        lax.fori_loop(1, 16, step, 0)

    def result(q, index):
        half = pl.ds((q % 2) * 128, 128)
        return up_out.at[index, half, :] if q < 2 else down_out.at[index, :, half]

    def own_result(q):
        return pltpu.make_async_copy(part.at[q], result(q, m), store_sem.at[q])

    def next_d(q):
        bytes_of(part.at[q, pl.ds(0, 120)], c_recv.at[q]).wait()

        def step(d, carry):
            _, device = group_peer(d)
            pltpu.make_async_remote_copy(
                src_ref=part.at[q], dst_ref=result(q, m),
                send_sem=d_send.at[q], recv_sem=d_recv.at[q],
                device_id=device, device_id_type=MESH,
            ).start()
            return carry

        lax.fori_loop(1, 8, step, 0)
        own_result(q).start()

    def finish(q):
        own_result(q).wait()
        seven = result(q, pl.ds(0, 7))
        bytes_of(seven, d_recv.at[q]).wait()
        bytes_of(seven, d_send.at[q]).wait()
        bytes_of(rec_a.at[q, pl.ds(0, 7)], a_send.at[q]).wait()
        bytes_of(rec_b.at[q, pl.ds(0, 15)], b_send.at[q]).wait()
        bytes_of(part.at[q, pl.ds(0, 120)], c_send.at[q]).wait()
        bytes_of_round(q, x_send).wait()

    def up_round(q):
        half = pl.ds((q % 2) * 128, 128)
        wait_round(q)

        def pair(i, carry):
            rows = pl.ds(i * 128, 128)
            pre = jnp.concatenate(
                [recv[q][tgt[2 * i]], recv[q][tgt[2 * i + 1]]], axis=0
            ).astype(F32)
            sig = jax.nn.sigmoid(pre)
            slope_s[rows, half] = sig * (1.0 + pre * (1.0 - sig))
            act_t[:, rows] = (pre * sig).T.astype(BF16)
            return carry

        lax.fori_loop(0, 16, pair, 0)

        def tile(i, carry):
            term = jnp.dot(
                act_t[...], cot_s[:, pl.ds(pl.multiple_of(i * 256, 256), 256)],
                preferred_element_type=F32,
            )
            quarter[q, 2 * i, 0:128] = term[:, 0:128]
            quarter[q, 2 * i + 1, 0:128] = term[:, 128:256]
            return carry

        lax.fori_loop(0, 4, tile, 0)
        for other in range(8):
            quarter[q, other, 128:136] = jnp.zeros((8, 128), F32)

    def down_round(q):
        half = pl.ds((q % 2) * 128, 128)
        wait_round(q)

        def pair(i, bias):
            rows = pl.ds(i * 128, 128)
            deep = jnp.concatenate(
                [recv[q][tgt[2 * i]], recv[q][tgt[2 * i + 1]]], axis=0
            ).astype(F32)
            grad = ((deep + x_s[rows, half]) * slope_s[rows, half]).astype(BF16)
            pg_s[rows, half] = grad
            return bias + jnp.sum(grad.astype(F32).reshape(16, 8, 128), axis=0)

        bias = lax.fori_loop(0, 16, pair, jnp.zeros((8, 128), F32))

        def tile(i, carry):
            term = jnp.dot(
                feat_t[pl.ds(i * 256, 256), :], pg_s[:, half], preferred_element_type=F32
            )
            quarter[q, 2 * i, 0:128] = term[0:128]
            quarter[q, 2 * i + 1, 0:128] = term[128:256]
            return carry

        lax.fori_loop(0, 4, tile, 0)
        for other in range(8):
            quarter[q, other, 128:136] = bias

    def fine_rows(first, last):
        def pair(i, carry):
            grads = jnp.dot(
                pg_s[pl.ds(i * 128, 128), :], wd_s[...], preferred_element_type=F32
            ).astype(BF16)
            stacked = jnp.concatenate(
                [grads[:, k * 128 : (k + 1) * 128] for k in range(8)], axis=0
            )
            sites = pl.ds(i * 384, 384)
            fine_s[sites, :] = jnp.dot(
                chosen[sites, :], stacked, preferred_element_type=F32
            ).astype(BF16)
            return carry

        lax.fori_loop(first, last, pair, 0)

    def fine_copy():
        return pltpu.make_async_copy(fine_s, fine_out, store_sem.at[4])

    up_round(0)
    start_a(0)
    start_round(2)
    next_b(0)
    up_round(1)
    start_a(1)
    start_round(3)
    next_c(0)
    next_d(0)
    next_b(1)
    down_round(2)
    start_a(2)
    next_c(1)
    next_b(2)
    next_d(1)
    down_round(3)
    start_a(3)
    next_c(2)
    fine_rows(0, 6)
    next_b(3)
    next_d(2)
    fine_rows(6, 11)
    next_c(3)
    fine_rows(11, 16)
    fine_copy().start()
    next_d(3)
    for q in range(4):
        finish(q)
    fine_copy().wait()


def on_device(
    fine_feats, out_grad, pre_act, deep_grad, down_weight, up_weight,
    block_owner, parent_slot, child_offset,
):
    devices = lax.axis_size("scene") * lax.axis_size("crop")
    sites = fine_feats.shape[1]
    scale = float(devices * sites) ** (-0.5)
    hbm = pl.BlockSpec(memory_space=pl.ANY)
    vmem = pl.BlockSpec(memory_space=pltpu.VMEM)
    dma = pltpu.SemaphoreType.DMA
    call = pl.pallas_call(
        functools.partial(level_kernel, scale),
        out_shape=(
            jax.ShapeDtypeStruct((sites, 128), BF16),
            jax.ShapeDtypeStruct((8, 128, 256), F32),
            jax.ShapeDtypeStruct((8, 256, 128), F32),
            jax.ShapeDtypeStruct((1, 256), F32),
        ),
        in_specs=[
            pl.BlockSpec(memory_space=pltpu.SMEM), vmem, vmem, hbm, hbm, hbm, hbm, vmem, vmem,
        ],
        out_specs=(hbm, hbm, hbm, vmem),
        scratch_shapes=[
            pltpu.SMEM((32,), jnp.int32),
            pltpu.VMEM((sites, 128), BF16),
            pltpu.VMEM((sites, 128), BF16),
            pltpu.VMEM((64, 64, 128), BF16),
            pltpu.VMEM((64, 64, 128), BF16),
            pltpu.VMEM((64, 64, 128), BF16),
            pltpu.VMEM((64, 64, 128), BF16),
            pltpu.VMEM((sites, 1024), BF16),
            pltpu.VMEM((2048, 1024), BF16),
            pltpu.VMEM((1024, 2048), BF16),
            pltpu.VMEM((2048, 256), F32),
            pltpu.VMEM((2048, 256), F32),
            pltpu.VMEM((128, 2048), BF16),
            pltpu.VMEM((2048, 256), BF16),
            pltpu.VMEM((1024, 256), BF16),
            pltpu.VMEM((256, 1024), BF16),
            pltpu.VMEM((sites, 128), BF16),
            pltpu.VMEM((4, 8, 136, 128), F32),
            pltpu.VMEM((4, 8, 136, 128), F32),
            pltpu.VMEM((4, 16, 16, 128), F32),
            pltpu.VMEM((4, 16, 16, 128), F32),
            pltpu.VMEM((4, 128, 128), F32),
            dma((2,)), dma((4,)), dma((4,)), dma((4,)),
            dma((4,)), dma((4,)), dma((4,)), dma((4,)),
            dma((4,)), dma((4,)), dma((4,)), dma((4,)), dma((5,)),
        ],
        compiler_params=pltpu.CompilerParams(
            collective_id=0, has_side_effects=True, vmem_limit_bytes=60 << 20
        ),
        cost_estimate=pl.CostEstimate(
            flops=12 * 10**9, bytes_accessed=16 * 10**6, transcendentals=10**6
        ),
    )
    fine, down, up, bias = call(
        block_owner.reshape(32),
        parent_slot.reshape(sites // 128, 128),
        child_offset.reshape(sites // 128, 128),
        fine_feats[0],
        out_grad[0],
        pre_act.reshape(64, 64, 256),
        deep_grad.reshape(64, 64, 256),
        down_weight,
        up_weight,
    )
    return fine[None], down, up, bias[0]


def solution(mesh):
    return jax.shard_map(
        on_device,
        mesh=mesh,
        in_specs=(
            P("crop", "scene", None),
            P("crop", "scene", None),
            P("crop", "scene", None, None, None, None),
            P("crop", "scene", None, None, None, None),
            P(),
            P(),
            P("crop", "scene", None),
            P("crop", "scene"),
            P("crop", "scene"),
        ),
        out_specs=(P("crop", "scene", None), P(), P(), P()),
        check_vma=False,
    )
```

time: 379 us -> 113 us (0.30)
  waiting for transfers between devices: 119 us -> 0 us
  Pallas kernels: 0 us -> 107 us
  blocking collectives: 83.9 us -> 0 us
  matrix products: 67.7 us -> 0 us
  local copies, waits for them, and re-layouts: 54.1 us -> 5.88 us
  starting transfers between devices: 24.2 us -> 0 us
  other arithmetic: 14 us -> 0 us
  between operations: 14.2 us -> 0.65 us
    pallas_call x0 -> x1, Pallas kernels: none -> 107 us  [on_device(): call(block_owner.reshape(32), parent_slot.reshape(sites // 128, 128), chi...]
    psum x1 -> x0, blocking collectives: 83.9 us -> none  [on_device(): lax.psum((up_term, down_term, bias_term), ('crop', 'scene'))]
    psum x1 -> x0, waiting for transfers between devices: 77.2 us -> none  [on_device(): lax.psum((up_term, down_term, bias_term), ('crop', 'scene'))]
    dot_general x10 -> x0, matrix products: 67.7 us -> none  [the longest x1 13.8 us: local_grads(): jnp.einsum('brs,brc->bsc', chooser, cotan, preferred_element_type=jnp.flo...]
    all_to_all x4 -> x0, waiting for transfers between devices: 42.2 us -> none  [the longest x1 34.4 us: on_device(): lax.all_to_all(cot_send, 'scene', split_axis=0, concat_axis=0, tiled=True)]
    reshape x4 -> x0, local copies, waits for them, and re-layouts: 40.6 us -> none  [the longest x1 13.3 us: local_grads(): slot_grads = slot_grads.reshape(block_total, parents_block * 8, width)]
    all_to_all x4 -> x0, starting transfers between devices: 24.1 us -> none  [the longest x1 8.59 us: on_device(): lax.all_to_all(place_send, 'scene', split_axis=0, concat_axis=0, tiled=True)]
    mul x3 -> x0, other arithmetic: 6.2 us -> none  [the longest x1 3.35 us: silu_parts(): sig_value * (1.0 + pre_float * (1.0 - sig_value))]
  transfers between devices with their start and end apart: 5 -> 0, of which waited for: 4 -> 0; matrix products, arithmetic and copies ran while one was open for 17% -> 0% of each run, Pallas kernels for 0% -> 0%
where the time goes in v1:
time: 113 us
  Pallas kernels  107 us (95%)
  local copies, waits for them, and re-layouts  5.88 us (5%)
    pallas_call x1, Pallas kernels, on_device(): call(block_owner.reshape(32), parent_slot.reshape(sites // 128, 128), chi...  107 us
    unnamed x10, local copies, waits for them, and re-layouts  5.88 us

profile of v1, /device:TPU:1, one launch (start us, length us, event | category | flops | bytes accessed | tf_op | source)
XLA Modules:
  0.0 113.1 jit_solution(13501165676004627335)
XLA Ops:
  0.6 106.5 %shard_map.120 = (bf16[6144,128]{1,0:T(8,128)(2,1)}, f32[8,128,256]{2,1,0:T(8,128)}, f32[8,256,128]{2,1,0:T(8,128)}, f32[1,256]{1,0:T(1,128)}) custom-call(s32[32]{0:T(128)} %bitcast.17, s32[48,128]{1,0:T(8,128)} %bitcast.15, s32[48,128]{1,0:T(8,128)} %bitcast.16, bf16[6144,128]{1,0:T(8,128)(2,1)} %bitcast.13, bf16[6144,128]{1,0:T(8,128)(2,1)} %bitcast.14, ...), custom_call_target="tpu_custom_call" | custom-call | flops 12000000000 | bytes 16000000 | tf_op jit(solution)/shard_map/pallas_call | solution.py:423
  107.2 0.0 copy-start.1
  107.2 2.7 %copy.17 = bf16[1,6144,128]{2,1,0:T(8,128)(2,1)} copy(bf16[1,6144,128]{2,1,0:T(8,128)(2,1)} %bitcast.9) | data formatting | bytes 3145728
  109.9 0.0 copy-done.1
  109.9 0.0 copy-start
  109.9 1.0 copy.18
  110.9 0.6 copy-done
  111.5 0.0 copy-start.2
  111.5 1.0 copy.19
  112.5 0.0 copy-done.2
  112.5 0.6 copy.20
Async XLA Ops:
  107.2 2.8 %copy-start.1 = (f32[8,128,256]{2,1,0:T(8,128)S(1)}, f32[8,128,256]{2,1,0:T(8,128)}, u32[]{:S(2)}) copy-start(f32[8,128,256]{2,1,0:T(8,128)} %get-tuple-element.17) | copy-start | bytes 3145732
  109.9 1.6 %copy-start = (f32[8,256,128]{2,1,0:T(8,128)S(1)}, f32[8,256,128]{2,1,0:T(8,128)}, u32[]{:S(2)}) copy-start(f32[8,256,128]{2,1,0:T(8,128)} %get-tuple-element.18) | copy-start | bytes 3145732
  111.5 1.0 copy-start.2

commit v2 on v1

--- a/solution.py
+++ b/solution.py
@@ -10,22 +10,21 @@
 MESH = pl.DeviceIdType.MESH
 BF16 = jnp.bfloat16
 F32 = jnp.float32
-NT = (((1,), (0,)), ((), ()))
 TN = (((0,), (0,)), ((), ()))
 
 CHIP_ORDER = (
     (2, 1), (1, 2), (2, 3), (3, 2), (2, 2), (2, 0), (0, 2),
     (1, 3), (3, 1), (1, 1), (3, 3), (1, 0), (0, 1), (3, 0), (0, 3),
 )
-UPFRONT = 2
+UPFRONT = 4
 
 
 def level_kernel(
     scale,
     owner_ref, pslot_ref, coff_ref, feats_hbm, cotan_hbm, pre_hbm, deep_hbm, wd_ref, wu_ref,
     fine_out, down_out, up_out, bias_out,
-    tgt, feats, cotan, recv0, recv1, recv2, recv3, chosen, cot_s, feat_t, x_s, slope_s, act_t, pg_s, wu_s, wd_s, fine_s,
-    quarter, rec_a, msg_b, rec_b, part, load_sem, own_sem, x_send, x_recv,
+    tgt, feats, cotan, recv0, recv1, recv2, recv3, chosen, cot_t, feat_t, x_s, slope_s, act_s, pg_s, wd_s, fine_s,
+    quarter, rec_a, msg_b, rec_b, part, rec_d, result, load_sem, own_sem, x_send, x_recv,
     a_send, a_recv, b_send, b_recv, c_send, c_recv, d_send, d_recv, store_sem,
 ):
     recv = (recv0, recv1, recv2, recv3)
@@ -122,50 +121,47 @@
     lax.fori_loop(0, 32, rank_block, 0)
 
     for k in range(8):
-        wu_s[pl.ds(k * 128, 128), :] = wu_ref[k].astype(F32).T.astype(BF16)
         wd_s[:, pl.ds(k * 128, 128)] = wd_ref[k].astype(F32).T.astype(BF16)
     for load in loads:
         load.wait()
 
     def place_pair(i, carry):
-        rows, cols = [], []
-        lane = lax.broadcasted_iota(jnp.int32, (1, 128), 1)
         for g in range(3):
             row = pl.ds(i * 3 + g, 1)
-            place = coff_ref[row, :] * 128 + pslot_ref[row, :]
-            if g == 1:
-                place = place + jnp.where(lane >= 64, 64, 0)
-            elif g == 2:
-                place = place + 64
-            sub = lax.broadcasted_iota(jnp.int32, (1024, 128), 0)
-            rows.append(jnp.where(sub == place, 1.0, 0.0).astype(BF16))
-            column = jnp.broadcast_to(place.astype(F32), (128, 128)).T
+            place = (coff_ref[row, :] * 64 + pslot_ref[row, :]).astype(F32)
+            column = jnp.broadcast_to(place, (128, 128)).T
             lanes = lax.broadcasted_iota(jnp.int32, (128, 128), 1).astype(F32)
-            for k in range(8):
+            for k in range(4):
                 chosen[pl.ds(i * 384 + g * 128, 128), pl.ds(k * 128, 128)] = jnp.where(
                     column == lanes + float(k * 128), 1.0, 0.0
                 ).astype(BF16)
-        sites = pl.ds(i * 384, 384)
+        turned = []
+        for half in range(2):
+            sites = pl.ds(i * 384 + half * 192, 192)
+            both = jnp.concatenate([feats[sites, :], cotan[sites, :]], axis=1)
+            turned.append(
+                lax.dot_general(
+                    both, chosen[sites, :], TN, preferred_element_type=F32
+                ).astype(BF16)
+            )
         parents = pl.ds(i * 128, 128)
-        chooser = jnp.concatenate(rows, axis=1)
-        placed = jnp.dot(chooser, cotan[sites, :], preferred_element_type=F32).astype(BF16)
         for k in range(8):
-            cot_s[parents, pl.ds(k * 128, 128)] = placed[k * 128 : (k + 1) * 128, :]
-        turned = lax.dot_general(
-            feats[sites, :], chosen[sites, :], TN, preferred_element_type=F32
-        ).astype(BF16)
-        for k in range(8):
-            feat_t[pl.ds(k * 128, 128), parents] = turned[:, k * 128 : (k + 1) * 128]
+            rows, lanes = pl.ds(k * 128, 128), slice(k * 64, (k + 1) * 64)
+            tile = jnp.concatenate([turned[0][:, lanes], turned[1][:, lanes]], axis=1)
+            feat_t[rows, parents] = tile[0:128]
+            cot_t[rows, parents] = tile[128:256]
         return carry
 
     lax.fori_loop(0, 16, place_pair, 0)
 
+    wu_t = jnp.concatenate([wu_ref[k] for k in range(8)], axis=1)
+
     def up_tile(i, carry):
-        rows = pl.ds(i * 512, 512)
-        x_s[rows, :] = jnp.dot(cot_s[rows, :], wu_s[...], preferred_element_type=F32)
+        rows = pl.ds(pl.multiple_of(i * 256, 256), 256)
+        x_s[rows, :] = jnp.dot(wu_t, cot_t[:, rows], preferred_element_type=F32).T
         return carry
 
-    lax.fori_loop(0, 4, up_tile, 0)
+    lax.fori_loop(0, 8, up_tile, 0)
 
     def start_a(q):
         def step(d, carry):
@@ -185,12 +181,13 @@
 
     def next_b(q):
         bytes_of(rec_a.at[q, pl.ds(0, 7)], a_recv.at[q]).wait()
-        total = rec_a[q, 0]
+        total = rec_a[q, 0].astype(F32)
         for other in range(1, 8):
-            total += rec_a[q, other]
+            total += rec_a[q, other].astype(F32)
+        bias = total[128:136] + total[136:144]
         for n in range(16):
             msg_b[q, n, 0:8] = total[n * 8 : (n + 1) * 8]
-            msg_b[q, n, 8:16] = total[128:136]
+            msg_b[q, n, 8:16] = bias
 
         def step(d, carry):
             other, device = chip_peer(d)
@@ -226,37 +223,48 @@
 
         lax.fori_loop(1, 16, step, 0)
 
-    def result(q, index):
-        half = pl.ds((q % 2) * 128, 128)
-        return up_out.at[index, half, :] if q < 2 else down_out.at[index, :, half]
-
-    def own_result(q):
-        return pltpu.make_async_copy(part.at[q], result(q, m), store_sem.at[q])
-
     def next_d(q):
         bytes_of(part.at[q, pl.ds(0, 120)], c_recv.at[q]).wait()
+        block = part[q].T if q < 2 else part[q]
+        rec_d[q, m] = block.astype(BF16)
 
         def step(d, carry):
             _, device = group_peer(d)
             pltpu.make_async_remote_copy(
-                src_ref=part.at[q], dst_ref=result(q, m),
+                src_ref=rec_d.at[q, m], dst_ref=rec_d.at[q, m],
                 send_sem=d_send.at[q], recv_sem=d_recv.at[q],
                 device_id=device, device_id_type=MESH,
             ).start()
             return carry
 
         lax.fori_loop(1, 8, step, 0)
-        own_result(q).start()
+
+    def store_copy(q):
+        half = pl.ds((q % 2) * 128, 128)
+        target = up_out.at[:, half, :] if q < 2 else down_out.at[:, :, half]
+        return pltpu.make_async_copy(result.at[q], target, store_sem.at[q])
+
+    def store(q):
+        bytes_of(rec_d.at[q, pl.ds(0, 7)], d_recv.at[q]).wait()
+        result[q] = rec_d[q].astype(F32)
+        store_copy(q).start()
 
     def finish(q):
-        own_result(q).wait()
-        seven = result(q, pl.ds(0, 7))
-        bytes_of(seven, d_recv.at[q]).wait()
-        bytes_of(seven, d_send.at[q]).wait()
+        store_copy(q).wait()
+        bytes_of(rec_d.at[q, pl.ds(0, 7)], d_send.at[q]).wait()
         bytes_of(rec_a.at[q, pl.ds(0, 7)], a_send.at[q]).wait()
         bytes_of(rec_b.at[q, pl.ds(0, 15)], b_send.at[q]).wait()
         bytes_of(part.at[q, pl.ds(0, 120)], c_send.at[q]).wait()
         bytes_of_round(q, x_send).wait()
+
+    def products(q, left, right):
+        def tile(i, carry):
+            term = jnp.dot(left[pl.ds(i * 256, 256), :], right, preferred_element_type=F32)
+            quarter[q, 2 * i, 0:128] = term[0:128].astype(BF16)
+            quarter[q, 2 * i + 1, 0:128] = term[128:256].astype(BF16)
+            return carry
+
+        lax.fori_loop(0, 4, tile, 0)
 
     def up_round(q):
         half = pl.ds((q % 2) * 128, 128)
@@ -269,23 +277,14 @@
             ).astype(F32)
             sig = jax.nn.sigmoid(pre)
             slope_s[rows, half] = sig * (1.0 + pre * (1.0 - sig))
-            act_t[:, rows] = (pre * sig).T.astype(BF16)
+            act_s[rows, :] = (pre * sig).astype(BF16)
             return carry
 
         lax.fori_loop(0, 16, pair, 0)
 
-        def tile(i, carry):
-            term = jnp.dot(
-                act_t[...], cot_s[:, pl.ds(pl.multiple_of(i * 256, 256), 256)],
-                preferred_element_type=F32,
-            )
-            quarter[q, 2 * i, 0:128] = term[:, 0:128]
-            quarter[q, 2 * i + 1, 0:128] = term[:, 128:256]
-            return carry
-
-        lax.fori_loop(0, 4, tile, 0)
+        products(q, cot_t, act_s[...])
         for other in range(8):
-            quarter[q, other, 128:136] = jnp.zeros((8, 128), F32)
+            quarter[q, other, 128:144] = jnp.zeros((16, 128), BF16)
 
     def down_round(q):
         half = pl.ds((q % 2) * 128, 128)
@@ -298,67 +297,64 @@
             ).astype(F32)
             grad = ((deep + x_s[rows, half]) * slope_s[rows, half]).astype(BF16)
             pg_s[rows, half] = grad
-            return bias + jnp.sum(grad.astype(F32).reshape(16, 8, 128), axis=0)
-
-        bias = lax.fori_loop(0, 16, pair, jnp.zeros((8, 128), F32))
-
-        def tile(i, carry):
-            term = jnp.dot(
-                feat_t[pl.ds(i * 256, 256), :], pg_s[:, half], preferred_element_type=F32
-            )
-            quarter[q, 2 * i, 0:128] = term[0:128]
-            quarter[q, 2 * i + 1, 0:128] = term[128:256]
-            return carry
-
-        lax.fori_loop(0, 4, tile, 0)
+            return bias + jnp.sum(grad.astype(F32).reshape(8, 16, 128), axis=0)
+
+        bias = lax.fori_loop(0, 16, pair, jnp.zeros((16, 128), F32))
+
+        products(q, feat_t, pg_s[:, half])
         for other in range(8):
-            quarter[q, other, 128:136] = bias
+            quarter[q, other, 128:144] = bias.astype(BF16)
 
     def fine_rows(first, last):
-        def pair(i, carry):
+        def four(i, carry):
             grads = jnp.dot(
-                pg_s[pl.ds(i * 128, 128), :], wd_s[...], preferred_element_type=F32
+                pg_s[pl.ds(i * 256, 256), :], wd_s[...], preferred_element_type=F32
             ).astype(BF16)
-            stacked = jnp.concatenate(
-                [grads[:, k * 128 : (k + 1) * 128] for k in range(8)], axis=0
-            )
-            sites = pl.ds(i * 384, 384)
-            fine_s[sites, :] = jnp.dot(
-                chosen[sites, :], stacked, preferred_element_type=F32
-            ).astype(BF16)
-            return carry
-
-        lax.fori_loop(first, last, pair, 0)
+            for j in range(4):
+                stacked = jnp.concatenate(
+                    [grads[j * 64 : (j + 1) * 64, k * 128 : (k + 1) * 128] for k in range(8)],
+                    axis=0,
+                )
+                sites = pl.ds(i * 768 + j * 192, 192)
+                fine_s[sites, :] = jnp.dot(
+                    chosen[sites, :], stacked, preferred_element_type=F32
+                ).astype(BF16)
+            return carry
+
+        lax.fori_loop(first, last, four, 0)
 
     def fine_copy():
         return pltpu.make_async_copy(fine_s, fine_out, store_sem.at[4])
 
     up_round(0)
     start_a(0)
-    start_round(2)
-    next_b(0)
     up_round(1)
     start_a(1)
-    start_round(3)
-    next_c(0)
-    next_d(0)
-    next_b(1)
     down_round(2)
     start_a(2)
+    next_b(0)
+    next_b(1)
+    down_round(3)
+    start_a(3)
+    next_c(0)
     next_c(1)
     next_b(2)
+    fine_rows(0, 2)
+    next_b(3)
+    next_c(2)
+    next_d(0)
     next_d(1)
-    down_round(3)
-    start_a(3)
-    next_c(2)
-    fine_rows(0, 6)
-    next_b(3)
+    fine_rows(2, 4)
+    next_c(3)
+    store(0)
     next_d(2)
-    fine_rows(6, 11)
-    next_c(3)
-    fine_rows(11, 16)
+    store(1)
+    fine_rows(4, 6)
+    next_d(3)
+    store(2)
+    fine_rows(6, 8)
     fine_copy().start()
-    next_d(3)
+    store(3)
     for q in range(4):
         finish(q)
     fine_copy().wait()
@@ -394,21 +390,22 @@
             pltpu.VMEM((64, 64, 128), BF16),
             pltpu.VMEM((64, 64, 128), BF16),
             pltpu.VMEM((64, 64, 128), BF16),
-            pltpu.VMEM((sites, 1024), BF16),
-            pltpu.VMEM((2048, 1024), BF16),
+            pltpu.VMEM((sites, 512), BF16),
+            pltpu.VMEM((1024, 2048), BF16),
             pltpu.VMEM((1024, 2048), BF16),
             pltpu.VMEM((2048, 256), F32),
             pltpu.VMEM((2048, 256), F32),
-            pltpu.VMEM((128, 2048), BF16),
+            pltpu.VMEM((2048, 128), BF16),
             pltpu.VMEM((2048, 256), BF16),
-            pltpu.VMEM((1024, 256), BF16),
             pltpu.VMEM((256, 1024), BF16),
             pltpu.VMEM((sites, 128), BF16),
-            pltpu.VMEM((4, 8, 136, 128), F32),
-            pltpu.VMEM((4, 8, 136, 128), F32),
+            pltpu.VMEM((4, 8, 144, 128), BF16),
+            pltpu.VMEM((4, 8, 144, 128), BF16),
             pltpu.VMEM((4, 16, 16, 128), F32),
             pltpu.VMEM((4, 16, 16, 128), F32),
             pltpu.VMEM((4, 128, 128), F32),
+            pltpu.VMEM((4, 8, 128, 128), BF16),
+            pltpu.VMEM((4, 8, 128, 128), F32),
             dma((2,)), dma((4,)), dma((4,)), dma((4,)),
             dma((4,)), dma((4,)), dma((4,)), dma((4,)),
             dma((4,)), dma((4,)), dma((4,)), dma((4,)), dma((5,)),

time: 113 us -> 90.4 us (0.80)
  Pallas kernels: 107 us -> 83.6 us
    pallas_call x1, Pallas kernels: 107 us -> 83.6 us  [on_device(): call(block_owner.reshape(32), parent_slot.reshape(sites // 128, 128), chi...]
where the time goes in v2:
time: 90.4 us; the launch traced here: 90.2 us
  Pallas kernels  83.6 us (92%)
  local copies, waits for them, and re-layouts  5.88 us (7%)
    pallas_call x1, Pallas kernels, on_device(): call(block_owner.reshape(32), parent_slot.reshape(sites // 128, 128), chi...  83.6 us
    unnamed x10, local copies, waits for them, and re-layouts  5.88 us

profile of v2, /device:TPU:1, one launch (start us, length us, event | category | flops | bytes accessed | tf_op | source)
XLA Modules:
  0.0 90.2 jit_solution(9034009572816547815)
XLA Ops:
  0.6 83.6 %shard_map.120 = (bf16[6144,128]{1,0:T(8,128)(2,1)}, f32[8,128,256]{2,1,0:T(8,128)}, f32[8,256,128]{2,1,0:T(8,128)}, f32[1,256]{1,0:T(1,128)}) custom-call(s32[32]{0:T(128)} %bitcast.17, s32[48,128]{1,0:T(8,128)} %bitcast.15, s32[48,128]{1,0:T(8,128)} %bitcast.16, bf16[6144,128]{1,0:T(8,128)(2,1)} %bitcast.13, bf16[6144,128]{1,0:T(8,128)(2,1)} %bitcast.14, ...), custom_call_target="tpu_custom_call" | custom-call | flops 12000000000 | bytes 16000000 | tf_op jit(solution)/shard_map/pallas_call | solution.py:420
  84.3 0.0 copy-start.1
  84.3 2.7 %copy.17 = bf16[1,6144,128]{2,1,0:T(8,128)(2,1)} copy(bf16[1,6144,128]{2,1,0:T(8,128)(2,1)} %bitcast.9) | data formatting | bytes 3145728
  87.0 0.0 copy-done.1
  87.0 0.0 copy-start
  87.0 1.0 %copy.18 = f32[8,128,256]{2,1,0:T(8,128)} copy(f32[8,128,256]{2,1,0:T(8,128)S(1)} %copy-done.1) | data formatting | bytes 2097152
  88.0 0.6 copy-done
  88.6 0.0 copy-start.2
  88.6 1.0 %copy.19 = f32[8,256,128]{2,1,0:T(8,128)} copy(f32[8,256,128]{2,1,0:T(8,128)S(1)} %copy-done) | data formatting | bytes 2097152
  89.6 0.0 copy-done.2
  89.6 0.6 copy.20
Async XLA Ops:
  84.3 2.8 %copy-start.1 = (f32[8,128,256]{2,1,0:T(8,128)S(1)}, f32[8,128,256]{2,1,0:T(8,128)}, u32[]{:S(2)}) copy-start(f32[8,128,256]{2,1,0:T(8,128)} %get-tuple-element.17) | copy-start | bytes 3145732
  87.0 1.6 %copy-start = (f32[8,256,128]{2,1,0:T(8,128)S(1)}, f32[8,256,128]{2,1,0:T(8,128)}, u32[]{:S(2)}) copy-start(f32[8,256,128]{2,1,0:T(8,128)} %get-tuple-element.18) | copy-start | bytes 3145732
  88.6 1.0 %copy-start.2 = (f32[1,256]{1,0:T(1,128)S(1)}, f32[1,256]{1,0:T(1,128)}, u32[]{:S(2)}) copy-start(f32[1,256]{1,0:T(1,128)} %get-tuple-element.11) | copy-start | bytes 3076

commit v3 on v2

--- a/solution.py
+++ b/solution.py
@@ -21,10 +21,10 @@
 
 def level_kernel(
     scale,
-    owner_ref, pslot_ref, coff_ref, feats_hbm, cotan_hbm, pre_hbm, deep_hbm, wd_ref, wu_ref,
-    fine_out, down_out, up_out, bias_out,
-    tgt, feats, cotan, recv0, recv1, recv2, recv3, chosen, cot_t, feat_t, x_s, slope_s, act_s, pg_s, wd_s, fine_s,
-    quarter, rec_a, msg_b, rec_b, part, rec_d, result, load_sem, own_sem, x_send, x_recv,
+    owner_ref, pslot_hbm, coff_hbm, feats_hbm, cotan_hbm, pre_hbm, deep_hbm, wd_hbm, wu_hbm,
+    fine_out, tiles_out, bias_out,
+    tgt, pslot_ref, coff_ref, wd_ref, wu_ref, feats, cotan, recv0, recv1, recv2, recv3, chosen, cot_t, feat_t, x_s, slope_s, act_s, pg_s, wd_s, fine_s,
+    quarter, rec_a, msg_b, rec_b, part, mine_s, load_sem, own_sem, x_send, x_recv,
     a_send, a_recv, b_send, b_recv, c_send, c_recv, d_send, d_recv, store_sem,
 ):
     recv = (recv0, recv1, recv2, recv3)
@@ -106,6 +106,10 @@
     loads = [
         pltpu.make_async_copy(cotan_hbm, cotan, load_sem.at[0]),
         pltpu.make_async_copy(feats_hbm, feats, load_sem.at[1]),
+        pltpu.make_async_copy(pslot_hbm, pslot_ref, load_sem.at[2]),
+        pltpu.make_async_copy(coff_hbm, coff_ref, load_sem.at[3]),
+        pltpu.make_async_copy(wd_hbm, wd_ref, load_sem.at[4]),
+        pltpu.make_async_copy(wu_hbm, wu_ref, load_sem.at[5]),
     ]
     for load in loads:
         load.start()
@@ -120,10 +124,10 @@
 
     lax.fori_loop(0, 32, rank_block, 0)
 
+    for load in loads:
+        load.wait()
     for k in range(8):
         wd_s[:, pl.ds(k * 128, 128)] = wd_ref[k].astype(F32).T.astype(BF16)
-    for load in loads:
-        load.wait()
 
     def place_pair(i, carry):
         for g in range(3):
@@ -223,35 +227,33 @@
 
         lax.fori_loop(1, 16, step, 0)
 
+    def own_tile(q):
+        return pltpu.make_async_copy(
+            mine_s.at[q], tiles_out.at[q, m], store_sem.at[q]
+        )
+
     def next_d(q):
         bytes_of(part.at[q, pl.ds(0, 120)], c_recv.at[q]).wait()
         block = part[q].T if q < 2 else part[q]
-        rec_d[q, m] = block.astype(BF16)
+        mine_s[q] = block.astype(BF16)
 
         def step(d, carry):
             _, device = group_peer(d)
             pltpu.make_async_remote_copy(
-                src_ref=rec_d.at[q, m], dst_ref=rec_d.at[q, m],
+                src_ref=mine_s.at[q], dst_ref=tiles_out.at[q, m],
                 send_sem=d_send.at[q], recv_sem=d_recv.at[q],
                 device_id=device, device_id_type=MESH,
             ).start()
             return carry
 
         lax.fori_loop(1, 8, step, 0)
-
-    def store_copy(q):
-        half = pl.ds((q % 2) * 128, 128)
-        target = up_out.at[:, half, :] if q < 2 else down_out.at[:, :, half]
-        return pltpu.make_async_copy(result.at[q], target, store_sem.at[q])
-
-    def store(q):
-        bytes_of(rec_d.at[q, pl.ds(0, 7)], d_recv.at[q]).wait()
-        result[q] = rec_d[q].astype(F32)
-        store_copy(q).start()
+        own_tile(q).start()
 
     def finish(q):
-        store_copy(q).wait()
-        bytes_of(rec_d.at[q, pl.ds(0, 7)], d_send.at[q]).wait()
+        own_tile(q).wait()
+        seven = tiles_out.at[q, pl.ds(0, 7)]
+        bytes_of(seven, d_recv.at[q]).wait()
+        bytes_of(seven, d_send.at[q]).wait()
         bytes_of(rec_a.at[q, pl.ds(0, 7)], a_send.at[q]).wait()
         bytes_of(rec_b.at[q, pl.ds(0, 15)], b_send.at[q]).wait()
         bytes_of(part.at[q, pl.ds(0, 120)], c_send.at[q]).wait()
@@ -336,25 +338,20 @@
     next_b(1)
     down_round(3)
     start_a(3)
+    next_b(2)
     next_c(0)
     next_c(1)
-    next_b(2)
     fine_rows(0, 2)
     next_b(3)
-    next_c(2)
     next_d(0)
     next_d(1)
-    fine_rows(2, 4)
+    next_c(2)
+    fine_rows(2, 3)
     next_c(3)
-    store(0)
     next_d(2)
-    store(1)
-    fine_rows(4, 6)
     next_d(3)
-    store(2)
-    fine_rows(6, 8)
+    fine_rows(3, 8)
     fine_copy().start()
-    store(3)
     for q in range(4):
         finish(q)
     fine_copy().wait()
@@ -374,16 +371,19 @@
         functools.partial(level_kernel, scale),
         out_shape=(
             jax.ShapeDtypeStruct((sites, 128), BF16),
-            jax.ShapeDtypeStruct((8, 128, 256), F32),
-            jax.ShapeDtypeStruct((8, 256, 128), F32),
+            jax.ShapeDtypeStruct((4, 8, 128, 128), BF16),
             jax.ShapeDtypeStruct((1, 256), F32),
         ),
         in_specs=[
-            pl.BlockSpec(memory_space=pltpu.SMEM), vmem, vmem, hbm, hbm, hbm, hbm, vmem, vmem,
+            pl.BlockSpec(memory_space=pltpu.SMEM), hbm, hbm, hbm, hbm, hbm, hbm, hbm, hbm,
         ],
-        out_specs=(hbm, hbm, hbm, vmem),
+        out_specs=(hbm, hbm, vmem),
         scratch_shapes=[
             pltpu.SMEM((32,), jnp.int32),
+            pltpu.VMEM((sites // 128, 128), jnp.int32),
+            pltpu.VMEM((sites // 128, 128), jnp.int32),
+            pltpu.VMEM((8, 128, 256), BF16),
+            pltpu.VMEM((8, 256, 128), BF16),
             pltpu.VMEM((sites, 128), BF16),
             pltpu.VMEM((sites, 128), BF16),
             pltpu.VMEM((64, 64, 128), BF16),
@@ -404,9 +404,8 @@
             pltpu.VMEM((4, 16, 16, 128), F32),
             pltpu.VMEM((4, 16, 16, 128), F32),
             pltpu.VMEM((4, 128, 128), F32),
-            pltpu.VMEM((4, 8, 128, 128), BF16),
-            pltpu.VMEM((4, 8, 128, 128), F32),
-            dma((2,)), dma((4,)), dma((4,)), dma((4,)),
+            pltpu.VMEM((4, 128, 128), BF16),
+            dma((6,)), dma((4,)), dma((4,)), dma((4,)),
             dma((4,)), dma((4,)), dma((4,)), dma((4,)),
             dma((4,)), dma((4,)), dma((4,)), dma((4,)), dma((5,)),
         ],
@@ -417,7 +416,7 @@
             flops=12 * 10**9, bytes_accessed=16 * 10**6, transcendentals=10**6
         ),
     )
-    fine, down, up, bias = call(
+    fine, tiles, bias = call(
         block_owner.reshape(32),
         parent_slot.reshape(sites // 128, 128),
         child_offset.reshape(sites // 128, 128),
@@ -428,6 +427,8 @@
         down_weight,
         up_weight,
     )
+    up = jnp.concatenate([tiles[0], tiles[1]], axis=1).astype(F32)
+    down = jnp.concatenate([tiles[2], tiles[3]], axis=2).astype(F32)
     return fine[None], down, up, bias[0]
 
 

time: 90.4 us -> 87.5 us (0.968)
  local copies, waits for them, and re-layouts: 5.88 us -> 3.01 us
  other arithmetic: 0 us -> 2.08 us
  Pallas kernels: 83.6 us -> 81.6 us
    unnamed x10 -> x6, local copies, waits for them, and re-layouts: 5.88 us -> 1.71 us
    convert_element_type x0 -> x2, other arithmetic: none -> 2.08 us  [the longest x1 1.04 us: on_device(): down = jnp.concatenate([tiles[2], tiles[3]], axis=2).astype(F32)]
    pallas_call x1, Pallas kernels: 83.6 us -> 81.6 us  [on_device(): call(block_owner.reshape(32), parent_slot.reshape(sites // 128, 128), chi...]
    squeeze x0 -> x1, local copies, waits for them, and re-layouts: none -> 1.29 us  [on_device(): up = jnp.concatenate([tiles[0], tiles[1]], axis=1).astype(F32)]
where the time goes in v3:
time: 87.5 us; the launch traced here: 87.3 us
  Pallas kernels  81.6 us (93%)
  local copies, waits for them, and re-layouts  3.01 us (3%)
  other arithmetic  2.08 us (2%)
    pallas_call x1, Pallas kernels, on_device(): call(block_owner.reshape(32), parent_slot.reshape(sites // 128, 128), chi...  81.6 us

profile of v3, /device:TPU:1, one launch (start us, length us, event | category | flops | bytes accessed | tf_op | source)
XLA Modules:
  0.0 87.3 jit_solution(12002360821308810443)
XLA Ops:
  0.6 81.6 %shard_map.120 = (bf16[6144,128]{1,0:T(8,128)(2,1)}, bf16[4,8,128,128]{3,2,1,0:T(8,128)(2,1)}, f32[1,256]{1,0:T(1,128)}) custom-call(s32[32]{0:T(128)} %bitcast.25, s32[48,128]{1,0:T(8,128)} %bitcast.23, s32[48,128]{1,0:T(8,128)} %bitcast.24, bf16[6144,128]{1,0:T(8,128)(2,1)} %bitcast.21, bf16[6144,128]{1,0:T(8,128)(2,1)} %bitcast.22, ...), custom_call_target="tpu_custom_call" | custom-call | flops 12000000000 | bytes 16000000 | tf_op jit(solution)/shard_map/pallas_call | solution.py:419
  82.2 1.3 %slice_bitcast_fusion.1 = (bf16[8,128,128]{2,1,0:T(8,128)(2,1)S(1)}, bf16[8,128,128]{2,1,0:T(8,128)(2,1)S(1)}, bf16[8,128,128]{2,1,0:T(8,128)(2,1)S(1)}, bf16[8,128,128]{2,1,0:T(8,128)(2,1)S(1)}) fusion(bf16[4,8,128,128]{3,2,1,0:T(8,128)(2,1)} %get-tuple-element.8), kind=kLoop, calls=%fused_computation.3 | loop fusion | bytes 2097152 | tf_op jit(solution)/shard_map/squeeze | solution.py:430
  83.5 0.0 copy-start
  83.5 1.0 %maximum_convert_fusion.1 = f32[8,256,128]{2,1,0:T(8,128)} fusion(bf16[8,128,128]{2,1,0:T(8,128)(2,1)S(1)} %get-tuple-element.11, bf16[8,128,128]{2,1,0:T(8,128)(2,1)S(1)} %get-tuple-element.10), kind=kLoop, calls=%fused_computation.1 | loop fusion | flops 1048576 | bytes 1572864 | tf_op jit(solution)/shard_map/convert_element_type | solution.py:430
  84.6 1.0 %maximum_convert_fusion = f32[8,128,256]{2,1,0:T(8,128)} fusion(bf16[8,128,128]{2,1,0:T(8,128)(2,1)S(1)} %get-tuple-element.12, bf16[8,128,128]{2,1,0:T(8,128)(2,1)S(1)} %get-tuple-element.13), kind=kLoop, calls=%fused_computation | loop fusion | flops 1048576 | bytes 1572864 | tf_op jit(solution)/shard_map/convert_element_type | solution.py:431
  85.6 0.0 copy-done
  85.6 0.0 copy-start.1
  85.6 1.1 %copy.15 = bf16[1,6144,128]{2,1,0:T(8,128)(2,1)} copy(bf16[1,6144,128]{2,1,0:T(8,128)(2,1)S(1)} %bitcast.17) | data formatting | bytes 3145728
  86.8 0.0 copy-done.1
  86.8 0.6 copy.16
Async XLA Ops:
  83.5 2.1 %copy-start = (bf16[6144,128]{1,0:T(8,128)(2,1)S(1)}, bf16[6144,128]{1,0:T(8,128)(2,1)}, u32[]{:S(2)}) copy-start(bf16[6144,128]{1,0:T(8,128)(2,1)} %get-tuple-element.7) | copy-start | bytes 4718596
  85.6 1.1 %copy-start.1 = (f32[1,256]{1,0:T(1,128)S(1)}, f32[1,256]{1,0:T(1,128)}, u32[]{:S(2)}) copy-start(f32[1,256]{1,0:T(1,128)} %get-tuple-element.9) | copy-start | bytes 3076

commit v4 on v3

--- a/solution.py
+++ b/solution.py
@@ -13,8 +13,8 @@
 TN = (((0,), (0,)), ((), ()))
 
 CHIP_ORDER = (
-    (2, 1), (1, 2), (2, 3), (3, 2), (2, 2), (2, 0), (0, 2),
-    (1, 3), (3, 1), (1, 1), (3, 3), (1, 0), (0, 1), (3, 0), (0, 3),
+    (2, 2), (2, 1), (1, 2), (2, 3), (3, 2), (1, 1), (3, 3),
+    (1, 3), (3, 1), (2, 0), (0, 2), (1, 0), (0, 1), (3, 0), (0, 3),
 )
 UPFRONT = 4
 
@@ -167,17 +167,14 @@
 
     lax.fori_loop(0, 8, up_tile, 0)
 
+    def send_a(q, other):
+        pltpu.make_async_remote_copy(
+            src_ref=quarter.at[q, other], dst_ref=rec_a.at[q, m],
+            send_sem=a_send.at[q], recv_sem=a_recv.at[q],
+            device_id=(other // 2, chip * 2 + other % 2), device_id_type=MESH,
+        ).start()
+
     def start_a(q):
-        def step(d, carry):
-            other, device = group_peer(d)
-            pltpu.make_async_remote_copy(
-                src_ref=quarter.at[q, other], dst_ref=rec_a.at[q, m],
-                send_sem=a_send.at[q], recv_sem=a_recv.at[q],
-                device_id=device, device_id_type=MESH,
-            ).start()
-            return carry
-
-        lax.fori_loop(1, 8, step, 0)
         rec_a[q, m] = quarter[q, m]
 
     def bytes_of(ref, sem):
@@ -264,6 +261,10 @@
             term = jnp.dot(left[pl.ds(i * 256, 256), :], right, preferred_element_type=F32)
             quarter[q, 2 * i, 0:128] = term[0:128].astype(BF16)
             quarter[q, 2 * i + 1, 0:128] = term[128:256].astype(BF16)
+            for other in (2 * i, 2 * i + 1):
+                @pl.when(other != m)
+                def _():
+                    send_a(q, other)
             return carry
 
         lax.fori_loop(0, 4, tile, 0)
@@ -284,9 +285,9 @@
 
         lax.fori_loop(0, 16, pair, 0)
 
-        products(q, cot_t, act_s[...])
         for other in range(8):
             quarter[q, other, 128:144] = jnp.zeros((16, 128), BF16)
+        products(q, cot_t, act_s[...])
 
     def down_round(q):
         half = pl.ds((q % 2) * 128, 128)
@@ -303,9 +304,9 @@
 
         bias = lax.fori_loop(0, 16, pair, jnp.zeros((16, 128), F32))
 
-        products(q, feat_t, pg_s[:, half])
         for other in range(8):
             quarter[q, other, 128:144] = bias.astype(BF16)
+        products(q, feat_t, pg_s[:, half])
 
     def fine_rows(first, last):
         def four(i, carry):

time: 87.5 us -> 86.8 us (level)
  no operation moved by 1% of the time
where the time goes in v4:
time: 86.8 us; the launch traced here: 86.6 us
  Pallas kernels  80.9 us (93%)
  local copies, waits for them, and re-layouts  3.01 us (3%)
  other arithmetic  2.08 us (2%)
    pallas_call x1, Pallas kernels, on_device(): call(block_owner.reshape(32), parent_slot.reshape(sites // 128, 128), chi...  80.9 us

profile of v4, /device:TPU:1, one launch (start us, length us, event | category | flops | bytes accessed | tf_op | source)
XLA Modules:
  0.0 86.6 jit_solution(11921186532111145950)
XLA Ops:
  0.6 80.9 %shard_map.120 = (bf16[6144,128]{1,0:T(8,128)(2,1)}, bf16[4,8,128,128]{3,2,1,0:T(8,128)(2,1)}, f32[1,256]{1,0:T(1,128)}) custom-call(s32[32]{0:T(128)} %bitcast.25, s32[48,128]{1,0:T(8,128)} %bitcast.23, s32[48,128]{1,0:T(8,128)} %bitcast.24, bf16[6144,128]{1,0:T(8,128)(2,1)} %bitcast.21, bf16[6144,128]{1,0:T(8,128)(2,1)} %bitcast.22, ...), custom_call_target="tpu_custom_call" | custom-call | flops 12000000000 | bytes 16000000 | tf_op jit(solution)/shard_map/pallas_call | solution.py:420
  81.5 1.3 %slice_bitcast_fusion.1 = (bf16[8,128,128]{2,1,0:T(8,128)(2,1)S(1)}, bf16[8,128,128]{2,1,0:T(8,128)(2,1)S(1)}, bf16[8,128,128]{2,1,0:T(8,128)(2,1)S(1)}, bf16[8,128,128]{2,1,0:T(8,128)(2,1)S(1)}) fusion(bf16[4,8,128,128]{3,2,1,0:T(8,128)(2,1)} %get-tuple-element.8), kind=kLoop, calls=%fused_computation.3 | loop fusion | bytes 2097152 | tf_op jit(solution)/shard_map/squeeze | solution.py:431
  82.8 0.0 copy-start
  82.8 1.0 %maximum_convert_fusion.1 = f32[8,256,128]{2,1,0:T(8,128)} fusion(bf16[8,128,128]{2,1,0:T(8,128)(2,1)S(1)} %get-tuple-element.11, bf16[8,128,128]{2,1,0:T(8,128)(2,1)S(1)} %get-tuple-element.10), kind=kLoop, calls=%fused_computation.1 | loop fusion | flops 1048576 | bytes 1572864 | tf_op jit(solution)/shard_map/convert_element_type | solution.py:431
  83.9 1.0 %maximum_convert_fusion = f32[8,128,256]{2,1,0:T(8,128)} fusion(bf16[8,128,128]{2,1,0:T(8,128)(2,1)S(1)} %get-tuple-element.12, bf16[8,128,128]{2,1,0:T(8,128)(2,1)S(1)} %get-tuple-element.13), kind=kLoop, calls=%fused_computation | loop fusion | flops 1048576 | bytes 1572864 | tf_op jit(solution)/shard_map/convert_element_type | solution.py:432
  84.9 0.0 copy-done
  84.9 0.0 copy-start.1
  84.9 1.1 %copy.15 = bf16[1,6144,128]{2,1,0:T(8,128)(2,1)} copy(bf16[1,6144,128]{2,1,0:T(8,128)(2,1)S(1)} %bitcast.17) | data formatting | bytes 3145728
  86.1 0.0 copy-done.1
  86.1 0.6 copy.16
Async XLA Ops:
  82.8 2.1 %copy-start = (bf16[6144,128]{1,0:T(8,128)(2,1)S(1)}, bf16[6144,128]{1,0:T(8,128)(2,1)}, u32[]{:S(2)}) copy-start(bf16[6144,128]{1,0:T(8,128)(2,1)} %get-tuple-element.7) | copy-start | bytes 4718596
  84.9 1.1 %copy-start.1 = (f32[1,256]{1,0:T(1,128)S(1)}, f32[1,256]{1,0:T(1,128)}, u32[]{:S(2)}) copy-start(f32[1,256]{1,0:T(1,128)} %get-tuple-element.9) | copy-start | bytes 3076

commit v5 on v4

--- a/solution.py
+++ b/solution.py
@@ -342,12 +342,11 @@
     next_b(2)
     next_c(0)
     next_c(1)
-    fine_rows(0, 2)
+    fine_rows(0, 3)
     next_b(3)
     next_d(0)
     next_d(1)
     next_c(2)
-    fine_rows(2, 3)
     next_c(3)
     next_d(2)
     next_d(3)

time: 86.8 us -> 86.8 us (level)
  no operation moved by 1% of the time
where the time goes in v5:
time: 86.8 us; the launch traced here: 86.6 us
  Pallas kernels  80.9 us (93%)
  local copies, waits for them, and re-layouts  3.01 us (3%)
  other arithmetic  2.08 us (2%)
    pallas_call x1, Pallas kernels, on_device(): call(block_owner.reshape(32), parent_slot.reshape(sites // 128, 128), chi...  80.9 us

profile of v5, /device:TPU:1, one launch (start us, length us, event | category | flops | bytes accessed | tf_op | source)
XLA Modules:
  0.0 86.6 jit_solution(8332756758836671150)
XLA Ops:
  0.6 80.9 %shard_map.120 = (bf16[6144,128]{1,0:T(8,128)(2,1)}, bf16[4,8,128,128]{3,2,1,0:T(8,128)(2,1)}, f32[1,256]{1,0:T(1,128)}) custom-call(s32[32]{0:T(128)} %bitcast.25, s32[48,128]{1,0:T(8,128)} %bitcast.23, s32[48,128]{1,0:T(8,128)} %bitcast.24, bf16[6144,128]{1,0:T(8,128)(2,1)} %bitcast.21, bf16[6144,128]{1,0:T(8,128)(2,1)} %bitcast.22, ...), custom_call_target="tpu_custom_call" | custom-call | flops 12000000000 | bytes 16000000 | tf_op jit(solution)/shard_map/pallas_call | solution.py:419
  81.5 1.3 %slice_bitcast_fusion.1 = (bf16[8,128,128]{2,1,0:T(8,128)(2,1)S(1)}, bf16[8,128,128]{2,1,0:T(8,128)(2,1)S(1)}, bf16[8,128,128]{2,1,0:T(8,128)(2,1)S(1)}, bf16[8,128,128]{2,1,0:T(8,128)(2,1)S(1)}) fusion(bf16[4,8,128,128]{3,2,1,0:T(8,128)(2,1)} %get-tuple-element.8), kind=kLoop, calls=%fused_computation.3 | loop fusion | bytes 2097152 | tf_op jit(solution)/shard_map/squeeze | solution.py:430
  82.8 0.0 copy-start
  82.8 1.0 %maximum_convert_fusion.1 = f32[8,256,128]{2,1,0:T(8,128)} fusion(bf16[8,128,128]{2,1,0:T(8,128)(2,1)S(1)} %get-tuple-element.11, bf16[8,128,128]{2,1,0:T(8,128)(2,1)S(1)} %get-tuple-element.10), kind=kLoop, calls=%fused_computation.1 | loop fusion | flops 1048576 | bytes 1572864 | tf_op jit(solution)/shard_map/convert_element_type | solution.py:430
  83.9 1.0 %maximum_convert_fusion = f32[8,128,256]{2,1,0:T(8,128)} fusion(bf16[8,128,128]{2,1,0:T(8,128)(2,1)S(1)} %get-tuple-element.12, bf16[8,128,128]{2,1,0:T(8,128)(2,1)S(1)} %get-tuple-element.13), kind=kLoop, calls=%fused_computation | loop fusion | flops 1048576 | bytes 1572864 | tf_op jit(solution)/shard_map/convert_element_type | solution.py:431
  84.9 0.0 copy-done
  84.9 0.0 copy-start.1
  84.9 1.1 %copy.15 = bf16[1,6144,128]{2,1,0:T(8,128)(2,1)} copy(bf16[1,6144,128]{2,1,0:T(8,128)(2,1)S(1)} %bitcast.17) | data formatting | bytes 3145728
  86.1 0.0 copy-done.1
  86.1 0.6 copy.16
Async XLA Ops:
  82.8 2.1 %copy-start = (bf16[6144,128]{1,0:T(8,128)(2,1)S(1)}, bf16[6144,128]{1,0:T(8,128)(2,1)}, u32[]{:S(2)}) copy-start(bf16[6144,128]{1,0:T(8,128)(2,1)} %get-tuple-element.7) | copy-start | bytes 4718596
  84.9 1.1 %copy-start.1 = (f32[1,256]{1,0:T(1,128)S(1)}, f32[1,256]{1,0:T(1,128)}, u32[]{:S(2)}) copy-start(f32[1,256]{1,0:T(1,128)} %get-tuple-element.9) | copy-start | bytes 3076
